TPU v7x, 32 devices: a whole 2x2x4 slice. The times are simulated.
32 devices in a mesh: row: 8 (over z, x), col: 4 (over y, core).
Axes of the slice: x: 2, y: 2, z: 4, core: 2. Of those that a mesh axis runs over, the one named last changes fastest.
Arguments:
- descriptors: float32 [512, 64], P(('row', 'col')), may hold values from -6 to 6, as said below
- preference: float32 [512], P(('row', 'col')), may hold values from -4 to -0.5
- responsibility: float32 [512, 512], P('row', 'col'), may hold values from -6 to 4, as said below
- availability: float32 [512, 512], P('row', 'col'), may hold values from -2 to 0, as said below
Outputs:
- resp_out: float32 [512, 512], P('row', 'col')
- avail_out: float32 [512, 512], P('row', 'col')
Inputs may be any that keep to these rules, and one draw needn't show every extreme that they name: `descriptors`: descriptors 64 m + 1, 64 m + 2 and 64 m + 3 are exact copies of descriptor 64 m (where they exist); the others are independent. `responsibility`: mostly negative; positive entries are rare and scattered over the columns. `availability`: columns 64 m + 1, 64 m + 2 and 64 m + 3 are exact copies of column 64 m (where they exist); the other entries are independent.
All inputs are finite; a program needn't handle non-finite values.
Results may differ from a plain program's by a relative error of at most 0.0003.
Values sent between devices are 32-bit elements; how exact they have to be, the bound alone decides.
A program may use at most 64 MiB of HBM per device.

v0:
```python
import jax
import jax.numpy as jnp
from jax import lax
from jax.sharding import PartitionSpec as P

ITERS = 3
DAMP = 0.5
NEG_FILL = -1e30


def local(descriptors, preference, responsibility, availability):
    tile_rows, tile_cols = responsibility.shape
    row_start = lax.axis_index("row") * tile_rows
    col_start = lax.axis_index("col") * tile_cols
    all_desc, all_pref = (
        lax.all_gather(descriptors, ("row", "col"), axis=0, tiled=True),
        lax.all_gather(preference, ("row", "col"), axis=0, tiled=True),
    )
    row_desc = lax.dynamic_slice_in_dim(all_desc, row_start, tile_rows, 0)
    row_pref = lax.dynamic_slice_in_dim(all_pref, row_start, tile_rows, 0)
    col_desc = lax.dynamic_slice_in_dim(all_desc, col_start, tile_cols, 0)
    width = descriptors.shape[1]
    row_norm = jnp.sum(row_desc * row_desc, 1)
    col_norm = jnp.sum(col_desc * col_desc, 1)
    cross = lax.dot_general(
        row_desc,
        col_desc,
        (((1,), (1,)), ((), ())),
        precision=lax.Precision.HIGHEST,
        preferred_element_type=jnp.float32,
    )
    similarity = (2.0 * cross - row_norm[:, None] - col_norm[None, :]) / width
    row_ids = row_start + jnp.arange(tile_rows, dtype=jnp.int32)
    col_ids = col_start + jnp.arange(tile_cols, dtype=jnp.int32)
    diag_mask = row_ids[:, None] == col_ids[None, :]
    similarity = jnp.where(diag_mask, row_pref[:, None], similarity)
    resp_now = responsibility
    avail_now = availability
    for step_index in range(ITERS):
        summed = avail_now + similarity
        best = lax.pmax(jnp.max(summed, 1), "col")
        at_best = summed == best[:, None]
        hits = lax.psum(jnp.sum(at_best, 1, dtype=jnp.float32), "col")
        below = lax.pmax(jnp.max(jnp.where(at_best, NEG_FILL, summed), 1), "col")
        runner = jnp.where(hits >= 2.0, best, below)
        excluded = jnp.where(at_best, runner[:, None], best[:, None])
        resp_now = DAMP * resp_now + (1.0 - DAMP) * (similarity - excluded)
        kept = jnp.where(diag_mask, resp_now, jnp.maximum(resp_now, 0.0))
        column = lax.psum(jnp.sum(kept, 0), "row")
        fresh = column[None, :] - kept
        fresh = jnp.where(diag_mask, fresh, jnp.minimum(fresh, 0.0))
        avail_now = DAMP * avail_now + (1.0 - DAMP) * fresh
    return (resp_now, avail_now)


def solution(mesh):
    placed = (P(("row", "col"), None), P(("row", "col")), P("row", "col"), P("row", "col"))
    return jax.shard_map(
        local,
        mesh=mesh,
        in_specs=placed,
        out_specs=(P("row", "col"), P("row", "col")),
        check_vma=False,
    )
```

profile of v0, /device:TPU:0, one launch (start us, length us, event | category | flops | bytes accessed | tf_op | source)
XLA Modules:
  0.0 194.8 jit_solution(9699927089328162763)
XLA Ops:
  0.7 0.6 copy-done.4
  1.3 0.2 dynamic-update-slice
  1.5 42.0 %all-reduce = f32[512]{0:T(512)S(1)} all-reduce(f32[512]{0:T(512)S(1)} %dynamic-update-slice), channel_id=1, replica_groups=mesh['row'=8,'col'=4] {'row','col'}, use_global_device_ids=true, to_apply=%add | all-reduce | flops 512 | bytes 4096
  43.5 40.9 %all_gather.7 = f32[512,64]{1,0:T(8,128)S(1)} all-gather(f32[16,64]{1,0:T(8,128)S(1)} %copy-done.3), channel_id=1, replica_groups=mesh['row'=8,'col'=4] {'row','col'}, dimensions={0}, use_global_device_ids=true | all-gather | bytes 135168 | tf_op jit(solution)/shard_map/all_gather | solution.py:16
  84.6 0.6 copy-done.1
  85.3 0.3 fusion.20
  85.6 6.0 %pmax.42 = f32[64]{0:T(128)S(1)} all-reduce(f32[64]{0:T(128)S(1)} %get-tuple-element.19), channel_id=1, replica_groups=mesh['row'=8,'col'=4] {'col'}, use_global_device_ids=true, to_apply=%region_3.4 | all-reduce | flops 64 | bytes 512 | tf_op jit(solution)/shard_map/pmax | solution.py:41
  91.6 0.2 convert_reduce_fusion.2
  91.8 5.7 %psum.42 = f32[64]{0:T(128)S(1)} all-reduce(f32[64]{0:T(128)S(1)} %get-tuple-element.6), channel_id=1, replica_groups=mesh['row'=8,'col'=4] {'col'}, use_global_device_ids=true, to_apply=%region_5.6 | all-reduce | flops 64 | bytes 512 | tf_op jit(solution)/shard_map/psum | solution.py:43
  97.5 6.7 %pmax.43 = f32[64]{0:T(128)S(1)} all-reduce(f32[64]{0:T(128)S(1)} %get-tuple-element.7), channel_id=1, replica_groups=mesh['row'=8,'col'=4] {'col'}, use_global_device_ids=true, to_apply=%region_7.8 | all-reduce | flops 64 | bytes 512 | tf_op jit(solution)/shard_map/pmax | solution.py:44
  104.3 17.1 %psum.43 = f32[128]{0:T(128)S(1)} all-reduce(f32[128]{0:T(128)S(1)} %fusion.13), channel_id=1, replica_groups=mesh['row'=8,'col'=4] {'row'}, use_global_device_ids=true, to_apply=%region_9.10 | all-reduce | flops 128 | bytes 1024 | tf_op jit(solution)/shard_map/psum | solution.py:49
  121.5 0.2 fusion.15
  121.7 5.7 %pmax.44 = f32[64]{0:T(128)S(1)} all-reduce(f32[64]{0:T(128)S(1)} %get-tuple-element.16), channel_id=1, replica_groups=mesh['row'=8,'col'=4] {'col'}, use_global_device_ids=true, to_apply=%region_11.12 | all-reduce | flops 64 | bytes 512 | tf_op jit(solution)/shard_map/pmax | solution.py:41
  127.3 0.2 convert_reduce_fusion.1
  127.5 6.1 %psum.44 = f32[64]{0:T(128)S(1)} all-reduce(f32[64]{0:T(128)S(1)} %get-tuple-element.4), channel_id=1, replica_groups=mesh['row'=8,'col'=4] {'col'}, use_global_device_ids=true, to_apply=%region_13.14 | all-reduce | flops 64 | bytes 512 | tf_op jit(solution)/shard_map/psum | solution.py:43
  133.6 5.6 %pmax.45 = f32[64]{0:T(128)S(1)} all-reduce(f32[64]{0:T(128)S(1)} %get-tuple-element.5), channel_id=1, replica_groups=mesh['row'=8,'col'=4] {'col'}, use_global_device_ids=true, to_apply=%region_15.16 | all-reduce | flops 64 | bytes 512 | tf_op jit(solution)/shard_map/pmax | solution.py:44
  139.4 19.1 %psum.45 = f32[128]{0:T(128)S(1)} all-reduce(f32[128]{0:T(128)S(1)} %get-tuple-element.13), channel_id=1, replica_groups=mesh['row'=8,'col'=4] {'row'}, use_global_device_ids=true, to_apply=%region_17.18 | all-reduce | flops 128 | bytes 1024 | tf_op jit(solution)/shard_map/psum | solution.py:49
  158.5 0.2 fusion.17
  158.7 5.7 %pmax.46 = f32[64]{0:T(128)S(1)} all-reduce(f32[64]{0:T(128)S(1)} %get-tuple-element.11), channel_id=1, replica_groups=mesh['row'=8,'col'=4] {'col'}, use_global_device_ids=true, to_apply=%region_19.20 | all-reduce | flops 64 | bytes 512 | tf_op jit(solution)/shard_map/pmax | solution.py:41
  164.4 0.2 convert_reduce_fusion
  164.6 6.7 %psum.46 = f32[64]{0:T(128)S(1)} all-reduce(f32[64]{0:T(128)S(1)} %get-tuple-element.2), channel_id=1, replica_groups=mesh['row'=8,'col'=4] {'col'}, use_global_device_ids=true, to_apply=%region_21.22 | all-reduce | flops 64 | bytes 512 | tf_op jit(solution)/shard_map/psum | solution.py:43
  171.2 5.6 %pmax.47 = f32[64]{0:T(128)S(1)} all-reduce(f32[64]{0:T(128)S(1)} %get-tuple-element.3), channel_id=1, replica_groups=mesh['row'=8,'col'=4] {'col'}, use_global_device_ids=true, to_apply=%region_23.24 | all-reduce | flops 64 | bytes 512 | tf_op jit(solution)/shard_map/pmax | solution.py:44
  177.0 17.1 %psum.47 = f32[128]{0:T(128)S(1)} all-reduce(f32[128]{0:T(128)S(1)} %get-tuple-element.8), channel_id=1, replica_groups=mesh['row'=8,'col'=4] {'row'}, use_global_device_ids=true, to_apply=%region_25.26 | all-reduce | flops 128 | bytes 1024 | tf_op jit(solution)/shard_map/psum | solution.py:49
  194.1 0.7 fusion.9
  (20 shorter events, 0.7 us)
Async XLA Ops:
  0.6 0.7 copy-start.4
  0.7 42.9 %copy-start.3 = (f32[16,64]{1,0:T(8,128)S(1)}, f32[16,64]{1,0:T(8,128)}, u32[]{:S(2)}) copy-start(f32[16,64]{1,0:T(8,128)} %param.4) | copy-start | bytes 12292
  84.5 0.8 copy-start.1
  85.6 18.6 %copy-start = (f32[64,128]{1,0:T(8,128)S(1)}, f32[64,128]{1,0:T(8,128)}, u32[]{:S(2)}) copy-start(f32[64,128]{1,0:T(8,128)} %param.6) | copy-start | bytes 98308
  177.0 17.8 %copy-start.2 = (f32[64,128]{1,0:T(8,128)}, f32[64,128]{1,0:T(8,128)S(1)}, u32[]{:S(2)}) copy-start(f32[64,128]{1,0:T(8,128)S(1)} %get-tuple-element.9) | copy-start | bytes 98308
where the time goes:
time: 195 us
  blocking collectives  190 us (97%)
  other arithmetic  2.18 us (1%)
    psum x3, blocking collectives, local(): column = lax.psum(jnp.sum(kept, 0), 'row')  53.4 us
    unnamed x1, blocking collectives  42 us
    all_gather x1, blocking collectives, local(): lax.all_gather(descriptors, ('row', 'col'), axis=0, tiled=True)  40.9 us
    psum x3, blocking collectives, local(): hits = lax.psum(jnp.sum(at_best, 1, dtype=jnp.float32), 'col')  18.5 us
    pmax x3, blocking collectives, local(): below = lax.pmax(jnp.max(jnp.where(at_best, NEG_FILL, summed), 1), 'col')  18 us
    pmax x3, blocking collectives, local(): best = lax.pmax(jnp.max(summed, 1), 'col')  17.3 us

commit v1 on v0

--- a/solution.py
+++ b/solution.py
@@ -8,12 +8,24 @@
 NEG_FILL = -1e30
 
 
+def collect(value, axis, dim):
+    ways, here = (lax.axis_size(axis), lax.axis_index(axis))
+    grown, reach = (value, 1)
+    while reach < ways:
+        theirs = lax.ppermute(grown, axis, [(d, d ^ reach) for d in range(ways)])
+        mine_first = jnp.concatenate([grown, theirs], axis=dim)
+        theirs_first = jnp.concatenate([theirs, grown], axis=dim)
+        grown = jnp.where(here & reach == 0, mine_first, theirs_first)
+        reach = 2 * reach
+    return grown
+
+
 def local(descriptors, preference, responsibility, availability):
     tile_rows, tile_cols = responsibility.shape
     row_start = lax.axis_index("row") * tile_rows
     col_start = lax.axis_index("col") * tile_cols
     all_desc, all_pref = (
-        lax.all_gather(descriptors, ("row", "col"), axis=0, tiled=True),
+        collect(descriptors, ("row", "col"), 0),
         lax.all_gather(preference, ("row", "col"), axis=0, tiled=True),
     )
     row_desc = lax.dynamic_slice_in_dim(all_desc, row_start, tile_rows, 0)

time: 195 us -> 177 us (0.908)
  blocking collectives: 190 us -> 151 us
  waiting for transfers between devices: 0 us -> 11.4 us
  starting transfers between devices: 0 us -> 8.9 us
    all_gather x1 -> x0, blocking collectives: 40.9 us -> none  [local(): lax.all_gather(descriptors, ('row', 'col'), axis=0, tiled=True)]
    ppermute x0 -> x5, waiting for transfers between devices: none -> 11.4 us  [collect(): theirs = lax.ppermute(grown, axis, [(d, d ^ reach) for d in range(ways)])]
    ppermute x0 -> x5, starting transfers between devices: none -> 8.9 us  [collect(): theirs = lax.ppermute(grown, axis, [(d, d ^ reach) for d in range(ways)])]
    psum x3, blocking collectives: 53.4 us -> 56.8 us  [local(): column = lax.psum(jnp.sum(kept, 0), 'row')]
  transfers between devices with their start and end apart: 0 -> 5, of which waited for: 0 -> 4; matrix products, arithmetic and copies ran while one was open for 0% -> 0% of each run, Pallas kernels for 0% -> 0%
where the time goes in v1:
time: 177 us; the launch traced here: 176 us
  blocking collectives  151 us (85%)
  waiting for transfers between devices  11.4 us (6%)
  starting transfers between devices  8.9 us (5%)
  other arithmetic  2.25 us (1%)
    psum x3, blocking collectives, local(): column = lax.psum(jnp.sum(kept, 0), 'row')  56.8 us
    unnamed x1, blocking collectives  40.4 us
    pmax x3, blocking collectives, local(): below = lax.pmax(jnp.max(jnp.where(at_best, NEG_FILL, summed), 1), 'col')  19.1 us
    pmax x3, blocking collectives, local(): best = lax.pmax(jnp.max(summed, 1), 'col')  17.3 us
    psum x3, blocking collectives, local(): hits = lax.psum(jnp.sum(at_best, 1, dtype=jnp.float32), 'col')  17.3 us
    ppermute x5, waiting for transfers between devices, collect(): theirs = lax.ppermute(grown, axis, [(d, d ^ reach) for d in range(ways)])  11.4 us
    ppermute x5, starting transfers between devices, collect(): theirs = lax.ppermute(grown, axis, [(d, d ^ reach) for d in range(ways)])  8.9 us
  transfers between devices with their start and end apart: 5, of which 4 were waited for; matrix products, arithmetic and copies ran while one was open for 0% of the time, Pallas kernels for 0%

profile of v1, /device:TPU:0, one launch (start us, length us, event | category | flops | bytes accessed | tf_op | source)
XLA Modules:
  0.0 176.0 jit_solution(3989884299848467819)
XLA Ops:
  1.1 1.0 collective-permute-done
  2.2 2.9 %collective-permute-start.1 = (f32[32,64]{1,0:T(8,128)S(1)}, f32[32,64]{1,0:T(8,128)S(1)}, u32[]{:S(2)}, u32[]{:S(2)}) collective-permute-start(f32[32,64]{1,0:T(8,128)S(1)} %maximum_select_fusion.4), channel_id=1, source_target_pairs={{0,2},{1,3},{2,0},{3,1},{4,6},{5,7},{6,4},{7,5},{8,10},{9,11},{10,... | collective-permute-start | bytes 24584 | tf_op jit(solution)/shard_map/ppermute | solution.py:15
  5.1 1.7 collective-permute-done.1
  6.8 2.0 %collective-permute-start.2 = (f32[64,64]{1,0:T(8,128)S(1)}, f32[64,64]{1,0:T(8,128)S(1)}, u32[]{:S(2)}, u32[]{:S(2)}) collective-permute-start(f32[64,64]{1,0:T(8,128)S(1)} %maximum_select_fusion.3), channel_id=1, source_target_pairs={{0,4},{1,5},{2,6},{3,7},{4,0},{5,1},{6,2},{7,3},{8,12},{9,13},{10,... | collective-permute-start | bytes 49160 | tf_op jit(solution)/shard_map/ppermute | solution.py:15
  8.8 1.9 %collective-permute-done.2 = f32[64,64]{1,0:T(8,128)S(1)} collective-permute-done((f32[64,64]{1,0:T(8,128)S(1)}, f32[64,64]{1,0:T(8,128)S(1)}, u32[]{:S(2)}, u32[]{:S(2)}) %collective-permute-start.2) | collective-permute-done | bytes 16416 | tf_op jit(solution)/shard_map/ppermute | solution.py:15
  10.8 2.1 %collective-permute-start.3 = (f32[128,64]{1,0:T(8,128)S(1)}, f32[128,64]{1,0:T(8,128)S(1)}, u32[]{:S(2)}, u32[]{:S(2)}) collective-permute-start(f32[128,64]{1,0:T(8,128)S(1)} %maximum_select_fusion.2), channel_id=1, source_target_pairs={{0,8},{1,9},{2,10},{3,11},{4,12},{5,13},{6,14},{7,15},{8,0},{9,1},... | collective-permute-start | bytes 98312 | tf_op jit(solution)/shard_map/ppermute | solution.py:15
  12.9 0.7 copy-done.4
  13.8 40.4 %all-reduce = f32[512]{0:T(512)S(1)} all-reduce(f32[512]{0:T(512)S(1)} %dynamic-update-slice), channel_id=1, replica_groups=mesh['row'=8,'col'=4] {'row','col'}, use_global_device_ids=true, to_apply=%add | all-reduce | flops 512 | bytes 4096
  54.3 1.3 collective-permute-start.4
  55.6 6.8 %collective-permute-done.4 = f32[256,64]{1,0:T(8,128)S(1)} collective-permute-done((f32[256,64]{1,0:T(8,128)S(1)}, f32[256,64]{1,0:T(8,128)S(1)}, u32[]{:S(2)}, u32[]{:S(2)}) %collective-permute-start.4) | collective-permute-done | bytes 65568 | tf_op jit(solution)/shard_map/ppermute | solution.py:15
  62.7 0.6 copy-done.1
  63.7 5.7 %pmax.42 = f32[64]{0:T(128)S(1)} all-reduce(f32[64]{0:T(128)S(1)} %get-tuple-element.19), channel_id=1, replica_groups=mesh['row'=8,'col'=4] {'col'}, use_global_device_ids=true, to_apply=%region_3.4 | all-reduce | flops 64 | bytes 512 | tf_op jit(solution)/shard_map/pmax | solution.py:53
  69.5 6.5 %pmax.43 = f32[64]{0:T(128)S(1)} all-reduce(f32[64]{0:T(128)S(1)} %get-tuple-element.7), channel_id=1, replica_groups=mesh['row'=8,'col'=4] {'col'}, use_global_device_ids=true, to_apply=%region_7.8 | all-reduce | flops 64 | bytes 512 | tf_op jit(solution)/shard_map/pmax | solution.py:56
  76.0 6.0 %psum.42 = f32[64]{0:T(128)S(1)} all-reduce(f32[64]{0:T(128)S(1)} %get-tuple-element.6), channel_id=1, replica_groups=mesh['row'=8,'col'=4] {'col'}, use_global_device_ids=true, to_apply=%region_5.6 | all-reduce | flops 64 | bytes 512 | tf_op jit(solution)/shard_map/psum | solution.py:55
  82.1 20.5 %psum.43 = f32[128]{0:T(128)S(1)} all-reduce(f32[128]{0:T(128)S(1)} %fusion.13), channel_id=1, replica_groups=mesh['row'=8,'col'=4] {'row'}, use_global_device_ids=true, to_apply=%region_9.10 | all-reduce | flops 128 | bytes 1024 | tf_op jit(solution)/shard_map/psum | solution.py:61
  102.9 5.9 %pmax.44 = f32[64]{0:T(128)S(1)} all-reduce(f32[64]{0:T(128)S(1)} %get-tuple-element.16), channel_id=1, replica_groups=mesh['row'=8,'col'=4] {'col'}, use_global_device_ids=true, to_apply=%region_11.12 | all-reduce | flops 64 | bytes 512 | tf_op jit(solution)/shard_map/pmax | solution.py:53
  109.0 5.8 %pmax.45 = f32[64]{0:T(128)S(1)} all-reduce(f32[64]{0:T(128)S(1)} %get-tuple-element.5), channel_id=1, replica_groups=mesh['row'=8,'col'=4] {'col'}, use_global_device_ids=true, to_apply=%region_15.16 | all-reduce | flops 64 | bytes 512 | tf_op jit(solution)/shard_map/pmax | solution.py:56
  114.7 5.6 %psum.44 = f32[64]{0:T(128)S(1)} all-reduce(f32[64]{0:T(128)S(1)} %get-tuple-element.4), channel_id=1, replica_groups=mesh['row'=8,'col'=4] {'col'}, use_global_device_ids=true, to_apply=%region_13.14 | all-reduce | flops 64 | bytes 512 | tf_op jit(solution)/shard_map/psum | solution.py:55
  120.5 17.1 %psum.45 = f32[128]{0:T(128)S(1)} all-reduce(f32[128]{0:T(128)S(1)} %get-tuple-element.13), channel_id=1, replica_groups=mesh['row'=8,'col'=4] {'row'}, use_global_device_ids=true, to_apply=%region_17.18 | all-reduce | flops 128 | bytes 1024 | tf_op jit(solution)/shard_map/psum | solution.py:61
  137.8 5.7 %pmax.46 = f32[64]{0:T(128)S(1)} all-reduce(f32[64]{0:T(128)S(1)} %get-tuple-element.11), channel_id=1, replica_groups=mesh['row'=8,'col'=4] {'col'}, use_global_device_ids=true, to_apply=%region_19.20 | all-reduce | flops 64 | bytes 512 | tf_op jit(solution)/shard_map/pmax | solution.py:53
  143.7 6.8 %pmax.47 = f32[64]{0:T(128)S(1)} all-reduce(f32[64]{0:T(128)S(1)} %get-tuple-element.3), channel_id=1, replica_groups=mesh['row'=8,'col'=4] {'col'}, use_global_device_ids=true, to_apply=%region_23.24 | all-reduce | flops 64 | bytes 512 | tf_op jit(solution)/shard_map/pmax | solution.py:56
  150.4 5.6 %psum.46 = f32[64]{0:T(128)S(1)} all-reduce(f32[64]{0:T(128)S(1)} %get-tuple-element.2), channel_id=1, replica_groups=mesh['row'=8,'col'=4] {'col'}, use_global_device_ids=true, to_apply=%region_21.22 | all-reduce | flops 64 | bytes 512 | tf_op jit(solution)/shard_map/psum | solution.py:55
  156.2 19.1 %psum.47 = f32[128]{0:T(128)S(1)} all-reduce(f32[128]{0:T(128)S(1)} %get-tuple-element.8), channel_id=1, replica_groups=mesh['row'=8,'col'=4] {'row'}, use_global_device_ids=true, to_apply=%region_25.26 | all-reduce | flops 128 | bytes 1024 | tf_op jit(solution)/shard_map/psum | solution.py:61
  175.3 0.7 fusion.9
  (34 shorter events, 2.7 us)
Async XLA Ops:
  0.6 1.6 collective-permute-start
  1.1 1.0 copy-start.3
  2.2 4.6 %collective-permute-start.1 = (f32[32,64]{1,0:T(8,128)S(1)}, f32[32,64]{1,0:T(8,128)S(1)}, u32[]{:S(2)}, u32[]{:S(2)}) collective-permute-start(f32[32,64]{1,0:T(8,128)S(1)} %maximum_select_fusion.4), channel_id=1, source_target_pairs={{0,2},{1,3},{2,0},{3,1},{4,6},{5,7},{6,4},{7,5},{8,10},{9,11},{10,... | collective-permute-start | bytes 24584 | tf_op jit(solution)/shard_map/ppermute | solution.py:15
  6.8 3.9 %collective-permute-start.2 = (f32[64,64]{1,0:T(8,128)S(1)}, f32[64,64]{1,0:T(8,128)S(1)}, u32[]{:S(2)}, u32[]{:S(2)}) collective-permute-start(f32[64,64]{1,0:T(8,128)S(1)} %maximum_select_fusion.3), channel_id=1, source_target_pairs={{0,4},{1,5},{2,6},{3,7},{4,0},{5,1},{6,2},{7,3},{8,12},{9,13},{10,... | collective-permute-start | bytes 49160 | tf_op jit(solution)/shard_map/ppermute | solution.py:15
  10.8 43.5 %collective-permute-start.3 = (f32[128,64]{1,0:T(8,128)S(1)}, f32[128,64]{1,0:T(8,128)S(1)}, u32[]{:S(2)}, u32[]{:S(2)}) collective-permute-start(f32[128,64]{1,0:T(8,128)S(1)} %maximum_select_fusion.2), channel_id=1, source_target_pairs={{0,8},{1,9},{2,10},{3,11},{4,12},{5,13},{6,14},{7,15},{8,0},{9,1},... | collective-permute-start | bytes 98312 | tf_op jit(solution)/shard_map/ppermute | solution.py:15
  12.9 0.7 copy-start.4
  54.3 8.1 %collective-permute-start.4 = (f32[256,64]{1,0:T(8,128)S(1)}, f32[256,64]{1,0:T(8,128)S(1)}, u32[]{:S(2)}, u32[]{:S(2)}) collective-permute-start(f32[256,64]{1,0:T(8,128)S(1)} %maximum_select_fusion.1), channel_id=1, source_target_pairs={{0,16},{1,17},{2,18},{3,19},{4,20},{5,21},{6,22},{7,23},{8,24},{9,... | collective-permute-start | bytes 196616 | tf_op jit(solution)/shard_map/ppermute | solution.py:15
  62.5 0.8 copy-start.1
  63.7 18.4 %copy-start = (f32[64,128]{1,0:T(8,128)S(1)}, f32[64,128]{1,0:T(8,128)}, u32[]{:S(2)}) copy-start(f32[64,128]{1,0:T(8,128)} %param.6) | copy-start | bytes 98308
  156.2 19.9 %copy-start.2 = (f32[64,128]{1,0:T(8,128)}, f32[64,128]{1,0:T(8,128)S(1)}, u32[]{:S(2)}) copy-start(f32[64,128]{1,0:T(8,128)S(1)} %get-tuple-element.9) | copy-start | bytes 98308
